TPU v7x, 1024 devices: a whole 4x4x32 slice. The times are simulated.
1024 devices in a mesh: expert: 32 (over y, x, core), dp: 32 (over z).
Axes of the slice: x: 4, y: 4, z: 32, core: 2. Of those that a mesh axis runs over, the one named last changes fastest.
Arguments:
- tokens: bfloat16 [32768, 1024], P(('expert', 'dp')), may hold values from -6 to 6
- expert_ids: int32 [32768, 8], P(('expert', 'dp')), may hold values from 0 to 63, all different within a row; in each aligned block of 32 rows (0 to 31, 32 to 63, ...) at most 8 rows name the same one
- gate_probs: float32 [32768, 8], P(('expert', 'dp')), may hold values from 0.05 to 0.4
- w_gate: bfloat16 [64, 1024, 384], P('expert'), may hold values from -0.1875 to 0.1875
- w_up: bfloat16 [64, 1024, 384], P('expert'), may hold values from -0.1875 to 0.1875
- w_down: bfloat16 [64, 384, 1024], P('expert'), may hold values from -0.3125 to 0.3125
- out_grad: bfloat16 [32768, 1024], P(('expert', 'dp')), may hold values from -24 to 24
Outputs:
- mixed: bfloat16 [32768, 1024], P(('expert', 'dp'))
- token_grad: bfloat16 [32768, 1024], P(('expert', 'dp'))
- down_grad: float32 [64, 384, 1024], P('expert', None, 'dp')
Inputs may be any that keep to these rules, and one draw needn't show every extreme that they name: `expert_ids`: in each aligned block of 32 rows (the rows of one device) no expert is named by more than 8 rows, a bound that some block reaches; the 8 experts of a row differ.
All inputs are finite; a program needn't handle non-finite values.
Results may differ from a plain program's by a relative error of at most 0.02.
Values may be sent and summed in bfloat16 or wider, within the bound.
A program may use at most 64 MiB of HBM per device.

v0:
```python
import jax
import jax.numpy as jnp
from jax import lax
from jax.sharding import PartitionSpec as P


def on_device(tokens, expert_ids, gate_probs, w_gate, w_up, w_down, out_grad):
    tok_dev, top = expert_ids.shape
    width = tokens.shape[1]
    exp_dev = w_gate.shape[0]
    hidden_units = w_gate.shape[2]
    groups = lax.axis_size("expert")
    experts = exp_dev * groups
    capacity = 2 * tok_dev * top // experts
    flat = expert_ids.reshape(-1)
    onehot = (flat[:, None] == jnp.arange(experts, dtype=jnp.int32)[None, :]).astype(jnp.int32)
    slot = jnp.sum((jnp.cumsum(onehot, 0) - 1) * onehot, 1)
    owner = flat // exp_dev
    local = flat % exp_dev
    position = local * (groups * capacity) + owner * capacity + slot
    row_tok = jnp.arange(tok_dev * top, dtype=jnp.int32) // top
    total_slots = exp_dev * groups * capacity
    probs = gate_probs.reshape(-1)[:, None]

    def place(rows):
        buffer = jnp.zeros((total_slots, width), jnp.bfloat16).at[position].set(rows)
        return buffer.reshape(exp_dev, groups, capacity, width)

    send_x = place(tokens[row_tok])
    send_dy = place((probs * out_grad.astype(jnp.float32)[row_tok]).astype(jnp.bfloat16))
    recv_x = lax.all_to_all(send_x, "expert", split_axis=1, concat_axis=1, tiled=True)
    recv_dy = None
    xin = recv_x.reshape(exp_dev, groups * capacity, width)
    gate_act = jnp.einsum("erd,edh->erh", xin, w_gate, preferred_element_type=jnp.float32)
    up_act = jnp.einsum("erd,edh->erh", xin, w_up, preferred_element_type=jnp.float32)
    sigma = jax.nn.sigmoid(gate_act)
    hidden = (gate_act * sigma * up_act).astype(jnp.bfloat16)
    outputs = jnp.einsum("erh,ehd->erd", hidden, w_down, preferred_element_type=jnp.float32).astype(
        jnp.bfloat16
    )
    returned = lax.all_to_all(
        outputs.reshape(exp_dev, groups, capacity, width),
        "expert",
        split_axis=1,
        concat_axis=1,
        tiled=True,
    )
    out_rows = returned.reshape(total_slots, width)[position].astype(jnp.float32)
    mixed = jnp.sum((probs * out_rows).reshape(tok_dev, top, width), 1).astype(jnp.bfloat16)
    recv_dy = lax.all_to_all(send_dy, "expert", split_axis=1, concat_axis=1, tiled=True)
    dyin = recv_dy.reshape(exp_dev, groups * capacity, width)
    hidden_grad = jnp.einsum("erd,ehd->erh", dyin, w_down, preferred_element_type=jnp.float32)
    partial_value = jnp.einsum(
        "erh,erd->ehd", hidden, dyin, preferred_element_type=jnp.float32
    ).astype(jnp.bfloat16)
    gate_grad = (hidden_grad * up_act * sigma * (1.0 + gate_act * (1.0 - sigma))).astype(
        jnp.bfloat16
    )
    up_grad = (hidden_grad * gate_act * sigma).astype(jnp.bfloat16)
    input_grad = (
        jnp.einsum("erh,edh->erd", gate_grad, w_gate, preferred_element_type=jnp.float32)
        + jnp.einsum("erh,edh->erd", up_grad, w_up, preferred_element_type=jnp.float32)
    ).astype(jnp.bfloat16)
    back = lax.all_to_all(
        input_grad.reshape(exp_dev, groups, capacity, width),
        "expert",
        split_axis=1,
        concat_axis=1,
        tiled=True,
    )
    grad_rows = back.reshape(total_slots, width)[position].astype(jnp.float32)
    token_grad = jnp.sum(grad_rows.reshape(tok_dev, top, width), 1).astype(jnp.bfloat16)
    data_groups = lax.axis_size("dp")
    share = width // data_groups
    pieces = partial_value.reshape(exp_dev, hidden_units, data_groups, share)
    received = lax.all_to_all(pieces, "dp", split_axis=2, concat_axis=2, tiled=True)
    down_grad = jnp.sum(received.astype(jnp.float32), 2)
    return (mixed, token_grad, down_grad)


def solution(mesh):
    return jax.shard_map(
        on_device,
        mesh=mesh,
        in_specs=(
            P(("expert", "dp"), None),
            P(("expert", "dp"), None),
            P(("expert", "dp"), None),
            P("expert", None, None),
            P("expert", None, None),
            P("expert", None, None),
            P(("expert", "dp"), None),
        ),
        out_specs=(P(("expert", "dp"), None), P(("expert", "dp"), None), P("expert", None, "dp")),
        check_vma=False,
    )
```

profile of v0, /device:TPU:14, one launch (start us, length us, event | category | flops | bytes accessed | tf_op | source)
XLA Modules:
  0.0 283.3 jit_solution(5176778853738844329)
XLA Ops:
  0.6 0.0 copy-start
  0.7 0.9 copy.36
  1.5 0.1 eq.31
  1.6 0.1 eq.27
  1.7 0.1 reshape.230
  1.8 0.6 reduce-window.6
  2.5 0.2 slice_reduce_fusion
  2.7 0.1 fusion.24
  2.8 0.0 copy-start.7
  2.8 4.8 %scatter_custom_fusion = bf16[512,1024]{1,0:T(8,128)(2,1)S(1)} fusion(s32[256]{0:T(256)S(1)} %bitcast.60, bf16[32,1024]{1,0:T(8,128)(2,1)} %param.7, s32[1024]{0:T(1024)S(1)} %pad_clamp_fusion.1, bf16[]{:T(256)} %constant.49.clone.1), kind=kCustom, calls=%fused_computation.32 | custom fusion | bytes 1049088 | tf_op jit(solution)/shard_map/scatter | solution.py:26
  7.7 0.0 copy-start.6
  7.7 1.1 copy.40
  8.8 0.0 copy-start.5
  8.8 17.5 %all-to-all-start = ((bf16[2,32,8,1024]{3,2,0,1:T(8,128)(2,1)}), bf16[2,32,8,1024]{3,2,0,1:T(8,128)(2,1)}, u32[]{:S(2)}, u32[]{:S(2)}) async-start(bf16[2,32,8,1024]{3,2,0,1:T(8,128)(2,1)} %copy.40), calls=%async_computation | async-start | bytes 2097152 | tf_op jit(solution)/shard_map/all_to_all | solution.py:31
  26.2 0.0 copy-done.6
  26.3 0.1 copy.35
  26.3 0.1 mul.81
  26.4 0.0 copy-done.5
  26.5 0.0 copy-done.7
  26.5 3.2 %scatter_custom_fusion.1 = bf16[512,1024]{1,0:T(8,128)(2,1)S(1)} fusion(s32[256]{0:T(256)S(1)} %bitcast.61, f32[256]{0:T(256)S(1)} %mul.81, bf16[]{:T(256)} %constant.49.clone.1, f32[32,1024]{1,0:T(8,128)S(1)} %convert_element_type.51, s32[1024]{0:T(1024)S(1)} %pad_clamp_fusion.1), kind=kCustom, calls=%fused_computation.30 | custom fusion | flops 524288 | bytes 1184770 | tf_op jit(solution)/shard_map/scatter | solution.py:26
  29.6 1.1 copy.45
  30.8 9.9 %all-to-all-done = bf16[2,32,8,1024]{3,2,0,1:T(8,128)(2,1)} async-done(((bf16[2,32,8,1024]{3,2,0,1:T(8,128)(2,1)}), bf16[2,32,8,1024]{3,2,0,1:T(8,128)(2,1)}, u32[]{:S(2)}, u32[]{:S(2)}) %all-to-all-start) | async-done | bytes 1048608 | tf_op jit(solution)/shard_map/all_to_all | solution.py:31
  40.6 6.9 %all-to-all-start.2 = ((bf16[2,32,8,1024]{3,2,0,1:T(8,128)(2,1)}), bf16[2,32,8,1024]{3,2,0,1:T(8,128)(2,1)S(1)}, u32[]{:S(2)}, u32[]{:S(2)}) async-start(bf16[2,32,8,1024]{3,2,0,1:T(8,128)(2,1)} %copy.45), calls=%async_computation.2 | async-start | bytes 2097152 | tf_op jit(solution)/shard_map/all_to_all | solution.py:50
  47.6 2.4 fusion.8
  50.0 0.0 copy-done
  50.0 0.0 copy-start.3
  50.0 0.0 copy-start.2
  50.0 3.2 %multiply_convert_fusion.3 = (bf16[2,256,384]{2,1,0:T(8,128)(2,1)S(1)}, f32[2,256,384]{2,1,0:T(8,128)}) fusion(f32[2,256,384]{2,1,0:T(8,128)S(1)} %fusion.8, bf16[2,1024,384]{2,1,0:T(8,128)(2,1)S(1)} %copy-done, bf16[2,32,8,1024]{3,2,0,1:T(8,128)(2,1)} %all-to-all-done), kind=kOutput, calls=%fused_computation.28 | convolution fusion | flops 403832832 | bytes 4587520 | tf_op jit(solution)/shard_map/erd,edh->erh/dot_general | solution.py:35
  53.2 0.0 copy-done.3
  53.2 0.0 copy-done.2
  53.2 0.7 fusion
  54.0 1.1 copy.42
  55.0 6.8 %all-to-all-done.2 = bf16[2,32,8,1024]{3,2,0,1:T(8,128)(2,1)S(1)} async-done(((bf16[2,32,8,1024]{3,2,0,1:T(8,128)(2,1)}), bf16[2,32,8,1024]{3,2,0,1:T(8,128)(2,1)S(1)}, u32[]{:S(2)}, u32[]{:S(2)}) %all-to-all-start.2) | async-done | bytes 1048608 | tf_op jit(solution)/shard_map/all_to_all | solution.py:50
  61.9 0.0 copy-start.1
  61.9 7.6 %all-to-all-start.1 = ((bf16[2,32,8,1024]{3,2,0,1:T(8,128)(2,1)}), bf16[2,32,8,1024]{3,2,0,1:T(8,128)(2,1)}, u32[]{:S(2)}, u32[]{:S(2)}) async-start(bf16[2,32,8,1024]{3,2,0,1:T(8,128)(2,1)} %copy.42), calls=%async_computation.1 | async-start | bytes 2097152 | tf_op jit(solution)/shard_map/all_to_all | solution.py:41
  69.5 0.0 copy-start.4
  69.5 0.0 copy-start.9
  69.5 0.0 copy-start.10
  69.5 2.3 fusion.4
  71.8 0.0 copy-done.1
  71.8 0.0 copy-done.4
  71.8 0.0 copy-done.9
  71.8 0.0 copy-done.10
  71.9 0.8 fusion.20
  72.7 0.8 fusion.1
  73.5 1.1 copy.47
  74.6 9.3 %all-to-all-done.1 = bf16[2,32,8,1024]{3,2,0,1:T(8,128)(2,1)} async-done(((bf16[2,32,8,1024]{3,2,0,1:T(8,128)(2,1)}), bf16[2,32,8,1024]{3,2,0,1:T(8,128)(2,1)}, u32[]{:S(2)}, u32[]{:S(2)}) %all-to-all-start.1) | async-done | bytes 1048608 | tf_op jit(solution)/shard_map/all_to_all | solution.py:41
  83.9 7.6 %all-to-all-start.3 = ((bf16[2,32,8,1024]{3,2,0,1:T(8,128)(2,1)}), bf16[2,32,8,1024]{3,2,0,1:T(8,128)(2,1)}, u32[]{:S(2)}, u32[]{:S(2)}) async-start(bf16[2,32,8,1024]{3,2,0,1:T(8,128)(2,1)} %copy.47), calls=%async_computation.3 | async-start | bytes 2097152 | tf_op jit(solution)/shard_map/all_to_all | solution.py:64
  91.5 1.8 convolution_convert_fusion
  93.3 1.6 copy.50
  94.9 2.9 %copy.51 = bf16[2,384,32,32]{1,3,0,2:T(8,128)(2,1)} copy(bf16[2,384,32,32]{1,3,2,0:T(8,128)(2,1)} %bitcast.56) | data formatting | bytes 3145728 | tf_op jit(solution)/shard_map/reshape | solution.py:75
  97.8 0.0 copy-start.8
  97.8 8.1 %all-to-all-done.3 = bf16[2,32,8,1024]{3,2,0,1:T(8,128)(2,1)} async-done(((bf16[2,32,8,1024]{3,2,0,1:T(8,128)(2,1)}), bf16[2,32,8,1024]{3,2,0,1:T(8,128)(2,1)}, u32[]{:S(2)}, u32[]{:S(2)}) %all-to-all-start.3) | async-done | bytes 1048608 | tf_op jit(solution)/shard_map/all_to_all | solution.py:64
  105.8 19.0 %all-to-all-start.4 = ((bf16[2,384,32,32]{1,3,0,2:T(8,128)(2,1)}), bf16[2,384,32,32]{1,3,0,2:T(8,128)(2,1)}, u32[]{:S(2)}, u32[]{:S(2)}) async-start(bf16[2,384,32,32]{1,3,0,2:T(8,128)(2,1)} %copy.51), calls=%async_computation.4 | async-start | bytes 3145728 | tf_op jit(solution)/shard_map/all_to_all | solution.py:76
  124.8 0.0 copy-done.8
  124.9 1.3 copy.43
  126.2 1.2 gather_fusion
  127.3 1.3 copy.48
  128.6 2.0 gather_fusion.1
  130.6 2.0 bitcast_reduce_fusion
  132.6 1.0 fusion.2
  133.6 147.4 %all-to-all-done.4 = bf16[2,384,32,32]{1,3,0,2:T(8,128)(2,1)} async-done(((bf16[2,384,32,32]{1,3,0,2:T(8,128)(2,1)}), bf16[2,384,32,32]{1,3,0,2:T(8,128)(2,1)}, u32[]{:S(2)}, u32[]{:S(2)}) %all-to-all-start.4) | async-done | bytes 1572896 | tf_op jit(solution)/shard_map/all_to_all | solution.py:76
  281.0 2.3 convert_reduce_fusion
  (8 shorter events, 0.1 us)
Async XLA Ops:
  0.6 49.4 %copy-start = (bf16[2,1024,384]{2,1,0:T(8,128)(2,1)S(1)}, bf16[2,1024,384]{2,1,0:T(8,128)(2,1)}, u32[]{:S(2)}) copy-start(bf16[2,1024,384]{2,1,0:T(8,128)(2,1)} %param.11) | copy-start | bytes 4718596
  2.8 23.6 %copy-start.7 = (s32[256,1]{0,1:T(1,128)}, s32[256,1]{0,1:T(1,128)S(1)}, u32[]{:S(2)}) copy-start(s32[256,1]{0,1:T(1,128)S(1)} %compare_select_fusion.1) | copy-start | bytes 3076
  7.7 18.6 %copy-start.6 = (f32[32,8]{0,1:T(8,128)S(1)}, f32[32,8]{0,1:T(8,128)}, u32[]{:S(2)}) copy-start(f32[32,8]{0,1:T(8,128)} %param.9) | copy-start | bytes 3076
  8.8 17.7 %copy-start.5 = (bf16[32,1024]{1,0:T(8,128)(2,1)S(1)}, bf16[32,1024]{1,0:T(8,128)(2,1)}, u32[]{:S(2)}) copy-start(bf16[32,1024]{1,0:T(8,128)(2,1)} %param.13) | copy-start | bytes 196612
  8.8 31.8 %all-to-all-start = ((bf16[2,32,8,1024]{3,2,0,1:T(8,128)(2,1)}), bf16[2,32,8,1024]{3,2,0,1:T(8,128)(2,1)}, u32[]{:S(2)}, u32[]{:S(2)}) async-start(bf16[2,32,8,1024]{3,2,0,1:T(8,128)(2,1)} %copy.40), calls=%async_computation | async-start | bytes 2097152 | tf_op jit(solution)/shard_map/all_to_all | solution.py:31
  40.6 21.3 %all-to-all-start.2 = ((bf16[2,32,8,1024]{3,2,0,1:T(8,128)(2,1)}), bf16[2,32,8,1024]{3,2,0,1:T(8,128)(2,1)S(1)}, u32[]{:S(2)}, u32[]{:S(2)}) async-start(bf16[2,32,8,1024]{3,2,0,1:T(8,128)(2,1)} %copy.45), calls=%async_computation.2 | async-start | bytes 2097152 | tf_op jit(solution)/shard_map/all_to_all | solution.py:50
  50.0 3.2 %copy-start.3 = (f32[2,256,384]{2,1,0:T(8,128)}, f32[2,256,384]{2,1,0:T(8,128)S(1)}, u32[]{:S(2)}) copy-start(f32[2,256,384]{2,1,0:T(8,128)S(1)} %fusion.8) | copy-start | bytes 2359300
  50.0 3.2 %copy-start.2 = (bf16[2,384,1024]{2,1,0:T(8,128)(2,1)S(1)}, bf16[2,384,1024]{2,1,0:T(8,128)(2,1)}, u32[]{:S(2)}) copy-start(bf16[2,384,1024]{2,1,0:T(8,128)(2,1)} %param.12) | copy-start | bytes 4718596
  61.9 9.9 %copy-start.1 = (bf16[2,32,8,1024]{3,2,0,1:T(8,128)(2,1)}, bf16[2,32,8,1024]{3,2,0,1:T(8,128)(2,1)S(1)}, u32[]{:S(2)}) copy-start(bf16[2,32,8,1024]{3,2,0,1:T(8,128)(2,1)S(1)} %all-to-all-done.2) | copy-start | bytes 3145732
  61.9 22.0 %all-to-all-start.1 = ((bf16[2,32,8,1024]{3,2,0,1:T(8,128)(2,1)}), bf16[2,32,8,1024]{3,2,0,1:T(8,128)(2,1)}, u32[]{:S(2)}, u32[]{:S(2)}) async-start(bf16[2,32,8,1024]{3,2,0,1:T(8,128)(2,1)} %copy.42), calls=%async_computation.1 | async-start | bytes 2097152 | tf_op jit(solution)/shard_map/all_to_all | solution.py:41
  69.5 2.3 copy-start.4
  69.5 2.3 copy-start.9
  69.5 2.3 copy-start.10
  83.9 22.0 %all-to-all-start.3 = ((bf16[2,32,8,1024]{3,2,0,1:T(8,128)(2,1)}), bf16[2,32,8,1024]{3,2,0,1:T(8,128)(2,1)}, u32[]{:S(2)}, u32[]{:S(2)}) async-start(bf16[2,32,8,1024]{3,2,0,1:T(8,128)(2,1)} %copy.47), calls=%async_computation.3 | async-start | bytes 2097152 | tf_op jit(solution)/shard_map/all_to_all | solution.py:64
  97.8 27.0 %copy-start.8 = (s32[256,1]{0,1:T(1,128)S(1)}, s32[256,1]{0,1:T(1,128)}, u32[]{:S(2)}) copy-start(s32[256,1]{0,1:T(1,128)} %copy-done.7) | copy-start | bytes 3076
  105.8 175.2 %all-to-all-start.4 = ((bf16[2,384,32,32]{1,3,0,2:T(8,128)(2,1)}), bf16[2,384,32,32]{1,3,0,2:T(8,128)(2,1)}, u32[]{:S(2)}, u32[]{:S(2)}) async-start(bf16[2,384,32,32]{1,3,0,2:T(8,128)(2,1)} %copy.51), calls=%async_computation.4 | async-start | bytes 3145728 | tf_op jit(solution)/shard_map/all_to_all | solution.py:76
where the time goes:
time: 284 us; the launch traced here: 283 us
  waiting for transfers between devices  181 us (64%)
  starting transfers between devices  58.6 us (21%)
  local copies, waits for them, and re-layouts  21 us (7%)
  matrix products  12 us (4%)
  other arithmetic  9.28 us (3%)
    all_to_all x1, waiting for transfers between devices, on_device(): lax.all_to_all(pieces, 'dp', split_axis=2, concat_axis=2, tiled=True)  147 us
    all_to_all x1, starting transfers between devices, on_device(): lax.all_to_all(pieces, 'dp', split_axis=2, concat_axis=2, tiled=True)  19 us
    all_to_all x1, starting transfers between devices, on_device(): lax.all_to_all(send_x, 'expert', split_axis=1, concat_axis=1, tiled=True)  17.5 us
    all_to_all x1, waiting for transfers between devices, on_device(): lax.all_to_all(send_x, 'expert', split_axis=1, concat_axis=1, tiled=True)  9.85 us
    all_to_all x1, waiting for transfers between devices, on_device(): lax.all_to_all(outputs.reshape(exp_dev, groups, capacity, width), 'expert...  9.29 us
    all_to_all x1, waiting for transfers between devices, on_device(): lax.all_to_all(input_grad.reshape(exp_dev, groups, capacity, width), 'exp...  8.05 us
    all_to_all x1, starting transfers between devices, on_device(): lax.all_to_all(outputs.reshape(exp_dev, groups, capacity, width), 'expert...  7.62 us
    all_to_all x1, starting transfers between devices, on_device(): lax.all_to_all(input_grad.reshape(exp_dev, groups, capacity, width), 'exp...  7.61 us
  transfers between devices with their start and end apart: 5, of which 5 were waited for; matrix products, arithmetic and copies ran while one was open for 11% of the time, Pallas kernels for 0%

commit v1 on v0

--- a/solution.py
+++ b/solution.py
@@ -1,7 +1,115 @@
 import jax
 import jax.numpy as jnp
 from jax import lax
+from jax.experimental import pallas as pl
+from jax.experimental.pallas import tpu as pltpu
 from jax.sharding import PartitionSpec as P
+
+MESH = pl.DeviceIdType.MESH
+
+
+def ring_kernel(n, p_ref, out_ref, sa, ra, sb, rb, sa_sem, ra_sem, sb_sem, rb_sem):
+    me = lax.axis_index("dp")
+    right, left = lax.rem(me + 1, n), lax.rem(me + n - 1, n)
+    half = n // 2
+    subs, _, cols = out_ref.shape
+    share = out_ref.shape[1]
+
+    def chunk(dest, sub):
+        return p_ref[
+            pl.ds(pl.multiple_of(dest * share, share), share), sub * cols : (sub + 1) * cols
+        ].astype(jnp.float32)
+
+    def up(step, sub):
+        return pltpu.make_async_remote_copy(
+            src_ref=sa.at[step, sub],
+            dst_ref=ra.at[step, sub],
+            send_sem=sa_sem.at[step, sub],
+            recv_sem=ra_sem.at[step, sub],
+            device_id={"dp": right},
+            device_id_type=MESH,
+        )
+
+    def down(step, sub):
+        return pltpu.make_async_remote_copy(
+            src_ref=sb.at[step, sub],
+            dst_ref=rb.at[step, sub],
+            send_sem=sb_sem.at[step, sub],
+            recv_sem=rb_sem.at[step, sub],
+            device_id={"dp": left},
+            device_id_type=MESH,
+        )
+
+    barrier = pltpu.get_barrier_semaphore()
+    for neighbour in (left, right):
+        pl.semaphore_signal(barrier, inc=1, device_id={"dp": neighbour}, device_id_type=MESH)
+    pl.semaphore_wait(barrier, 2)
+
+    def up_dest(step):
+        return lax.rem(me + half - step, n)
+
+    def down_dest(step):
+        return lax.rem(me + n - (half - 1) + step, n)
+
+    for sub in range(subs):
+        sa[0, sub] = chunk(up_dest(0), sub).astype(sa.dtype)
+        up(0, sub).start()
+        sb[0, sub] = chunk(down_dest(0), sub).astype(sb.dtype)
+        down(0, sub).start()
+
+    def step(s, carry):
+        for sub in range(subs):
+            up(s - 1, sub).wait_recv()
+            sa[s, sub] = (ra[s - 1, sub].astype(jnp.float32) + chunk(up_dest(s), sub)).astype(sa.dtype)
+            up(s, sub).start()
+            down(s - 1, sub).wait_recv()
+            sb[s, sub] = (rb[s - 1, sub].astype(jnp.float32) + chunk(down_dest(s), sub)).astype(sb.dtype)
+            down(s, sub).start()
+        return carry
+
+    lax.fori_loop(1, half - 1, step, 0)
+    last = half - 1
+    for sub in range(subs):
+        up(last - 1, sub).wait_recv()
+        sa[last, sub] = (ra[last - 1, sub].astype(jnp.float32) + chunk(up_dest(last), sub)).astype(sa.dtype)
+        up(last, sub).start()
+    for sub in range(subs):
+        down(last - 1, sub).wait_recv()
+        up(last, sub).wait_recv()
+        out_ref[sub] = (
+            chunk(me, sub)
+            + ra[last, sub].astype(jnp.float32)
+            + rb[last - 1, sub].astype(jnp.float32)
+        )
+
+    def drain(s, carry):
+        for sub in range(subs):
+            up(s, sub).wait_send()
+            down(s, sub).wait_send()
+        return carry
+
+    lax.fori_loop(0, half - 1, drain, 0)
+    for sub in range(subs):
+        up(last, sub).wait_send()
+
+
+def ring_sum(partial, n, subs):
+    width, cols = partial.shape
+    share = width // n
+    half = n // 2
+    slots = pltpu.VMEM((half, subs, share, cols // subs), jnp.bfloat16)
+    fewer = pltpu.VMEM((half - 1, subs, share, cols // subs), jnp.bfloat16)
+    sems = pltpu.SemaphoreType.DMA((half, subs))
+    return pl.pallas_call(
+        lambda *refs: ring_kernel(n, *refs),
+        out_shape=jax.ShapeDtypeStruct((subs, share, cols // subs), jnp.float32),
+        in_specs=[pl.BlockSpec(memory_space=pltpu.VMEM)],
+        out_specs=pl.BlockSpec(memory_space=pltpu.VMEM),
+        scratch_shapes=[slots, slots, fewer, fewer, sems, sems, sems, sems],
+        compiler_params=pltpu.CompilerParams(
+            collective_id=0, has_side_effects=True, vmem_limit_bytes=32 * 1024 * 1024
+        ),
+    )(partial)
 
 
 def on_device(tokens, expert_ids, gate_probs, w_gate, w_up, w_down, out_grad):
@@ -50,9 +158,18 @@
     recv_dy = lax.all_to_all(send_dy, "expert", split_axis=1, concat_axis=1, tiled=True)
     dyin = recv_dy.reshape(exp_dev, groups * capacity, width)
     hidden_grad = jnp.einsum("erd,ehd->erh", dyin, w_down, preferred_element_type=jnp.float32)
-    partial_value = jnp.einsum(
-        "erh,erd->ehd", hidden, dyin, preferred_element_type=jnp.float32
-    ).astype(jnp.bfloat16)
+    partial_value = jnp.concatenate(
+        [
+            jnp.einsum("rd,rh->dh", dyin[e], hidden[e], preferred_element_type=jnp.float32).astype(
+                jnp.bfloat16
+            )
+            for e in range(exp_dev)
+        ],
+        axis=1,
+    )
+    down_grad = jnp.transpose(
+        ring_sum(partial_value, lax.axis_size("dp"), exp_dev), (0, 2, 1)
+    )
     gate_grad = (hidden_grad * up_act * sigma * (1.0 + gate_act * (1.0 - sigma))).astype(
         jnp.bfloat16
     )
@@ -70,11 +187,6 @@
     )
     grad_rows = back.reshape(total_slots, width)[position].astype(jnp.float32)
     token_grad = jnp.sum(grad_rows.reshape(tok_dev, top, width), 1).astype(jnp.bfloat16)
-    data_groups = lax.axis_size("dp")
-    share = width // data_groups
-    pieces = partial_value.reshape(exp_dev, hidden_units, data_groups, share)
-    received = lax.all_to_all(pieces, "dp", split_axis=2, concat_axis=2, tiled=True)
-    down_grad = jnp.sum(received.astype(jnp.float32), 2)
     return (mixed, token_grad, down_grad)
 
 

time: 284 us -> 162 us (0.57)
  the two profiles are of different devices: /device:TPU:14 before, /device:TPU:2 now
where the time goes in v1:
time: 162 us; the launch traced here: 161 us
  Pallas kernels  60.2 us (37%)
  starting transfers between devices  33.4 us (21%)
  waiting for transfers between devices  31.6 us (20%)
  local copies, waits for them, and re-layouts  16.3 us (10%)
  matrix products  12.3 us (8%)
  other arithmetic  6.08 us (4%)
    pallas_call x1, Pallas kernels, ring_sum(): pl.pallas_call(lambda *refs: ring_kernel(n, *refs), out_shape=jax.ShapeDt...  60.2 us
    all_to_all x1, starting transfers between devices, on_device(): lax.all_to_all(send_x, 'expert', split_axis=1, concat_axis=1, tiled=True)  17.6 us
    all_to_all x1, waiting for transfers between devices, on_device(): lax.all_to_all(send_x, 'expert', split_axis=1, concat_axis=1, tiled=True)  11.8 us
    all_to_all x1, waiting for transfers between devices, on_device(): lax.all_to_all(outputs.reshape(exp_dev, groups, capacity, width), 'expert...  10.8 us
    all_to_all x1, waiting for transfers between devices, on_device(): lax.all_to_all(send_dy, 'expert', split_axis=1, concat_axis=1, tiled=True)  8.99 us
    all_to_all x1, starting transfers between devices, on_device(): lax.all_to_all(input_grad.reshape(exp_dev, groups, capacity, width), 'exp...  5.7 us
    all_to_all x1, starting transfers between devices, on_device(): lax.all_to_all(outputs.reshape(exp_dev, groups, capacity, width), 'expert...  5.05 us
    scatter x1, local copies, waits for them, and re-layouts, place(): jnp.zeros((total_slots, width), jnp.bfloat16).at[position].set(rows)  5.05 us
  transfers between devices with their start and end apart: 4, of which 3 were waited for; matrix products, arithmetic and copies ran while one was open for 13% of the time, Pallas kernels for 37%

profile of v1, /device:TPU:2, one launch (start us, length us, event | category | flops | bytes accessed | tf_op | source)
XLA Modules:
  0.0 160.9 jit_solution(12273310819527870114)
XLA Ops:
  0.6 0.0 copy-start
  0.7 0.9 copy.36
  1.5 0.1 eq.31
  1.6 0.1 eq.27
  1.7 0.1 reshape.231
  1.8 0.6 reduce-window.6
  2.5 0.2 slice_reduce_fusion
  2.7 0.1 fusion.22
  2.8 5.0 %scatter_custom_fusion = bf16[512,1024]{1,0:T(8,128)(2,1)S(1)} fusion(s32[256]{0:T(256)S(1)} %bitcast.69, bf16[32,1024]{1,0:T(8,128)(2,1)} %param.7, s32[1024]{0:T(1024)S(1)} %pad_clamp_fusion.1, bf16[]{:T(256)} %constant.49.clone.1), kind=kCustom, calls=%fused_computation.33 | custom fusion | bytes 1049088 | tf_op jit(solution)/shard_map/scatter | solution.py:134
  7.9 0.0 copy-start.9
  7.9 1.1 copy.40
  9.0 0.0 copy-start.8
  9.0 17.6 %all-to-all-start = ((bf16[2,32,8,1024]{3,2,0,1:T(8,128)(2,1)}), bf16[2,32,8,1024]{3,2,0,1:T(8,128)(2,1)}, u32[]{:S(2)}, u32[]{:S(2)}) async-start(bf16[2,32,8,1024]{3,2,0,1:T(8,128)(2,1)} %copy.40), calls=%async_computation | async-start | bytes 2097152 | tf_op jit(solution)/shard_map/all_to_all | solution.py:139
  26.5 0.0 copy-done.9
  26.5 0.1 copy.35
  26.6 0.1 mul.81
  26.7 0.0 copy-done.8
  26.7 3.2 %scatter_custom_fusion.1 = bf16[512,1024]{1,0:T(8,128)(2,1)S(1)} fusion(s32[256]{0:T(256)S(1)} %bitcast.70, f32[256]{0:T(256)S(1)} %mul.81, bf16[]{:T(256)} %constant.49.clone.1, f32[32,1024]{1,0:T(8,128)S(1)} %convert_element_type.51, s32[1024]{0:T(1024)S(1)} %pad_clamp_fusion.1), kind=kCustom, calls=%fused_computation.29 | custom fusion | flops 524288 | bytes 1184770 | tf_op jit(solution)/shard_map/scatter | solution.py:134
  29.9 1.1 copy.45
  31.0 11.8 %all-to-all-done = bf16[2,32,8,1024]{3,2,0,1:T(8,128)(2,1)} async-done(((bf16[2,32,8,1024]{3,2,0,1:T(8,128)(2,1)}), bf16[2,32,8,1024]{3,2,0,1:T(8,128)(2,1)}, u32[]{:S(2)}, u32[]{:S(2)}) %all-to-all-start) | async-done | bytes 1048608 | tf_op jit(solution)/shard_map/all_to_all | solution.py:139
  42.8 5.0 %all-to-all-start.2 = ((bf16[2,32,8,1024]{3,2,0,1:T(8,128)(2,1)}), bf16[2,32,8,1024]{3,2,0,1:T(8,128)(2,1)S(1)}, u32[]{:S(2)}, u32[]{:S(2)}) async-start(bf16[2,32,8,1024]{3,2,0,1:T(8,128)(2,1)} %copy.45), calls=%async_computation.2 | async-start | bytes 2097152 | tf_op jit(solution)/shard_map/all_to_all | solution.py:158
  47.9 2.4 %fusion.7 = f32[2,256,384]{2,1,0:T(8,128)S(1)} fusion(bf16[2,1024,384]{2,1,0:T(8,128)(2,1)} %param.10, bf16[2,32,8,1024]{3,2,0,1:T(8,128)(2,1)} %all-to-all-done), kind=kOutput, calls=%fused_computation.19 | convolution fusion | flops 402653184 | bytes 3407872 | tf_op jit(solution)/shard_map/erd,edh->erh/dot_general | solution.py:142
  50.3 0.0 copy-done
  50.3 0.0 copy-start.3
  50.3 2.9 %multiply_convert_fusion.3 = (bf16[2,256,384]{2,1,0:T(8,128)(2,1)S(1)}, f32[2,256,384]{2,1,0:T(8,128)}) fusion(f32[2,256,384]{2,1,0:T(8,128)S(1)} %fusion.7, bf16[2,1024,384]{2,1,0:T(8,128)(2,1)S(1)} %copy-done, bf16[2,32,8,1024]{3,2,0,1:T(8,128)(2,1)} %all-to-all-done), kind=kOutput, calls=%fused_computation.27 | convolution fusion | flops 403832832 | bytes 4587520 | tf_op jit(solution)/shard_map/erd,edh->erh/dot_general | solution.py:143
  53.3 0.0 copy-start.6
  53.3 0.0 copy-done.3
  53.3 0.7 fusion
  54.0 0.0 copy-done.6
  54.0 1.1 copy.42
  55.1 9.0 %all-to-all-done.2 = bf16[2,32,8,1024]{3,2,0,1:T(8,128)(2,1)S(1)} async-done(((bf16[2,32,8,1024]{3,2,0,1:T(8,128)(2,1)}), bf16[2,32,8,1024]{3,2,0,1:T(8,128)(2,1)S(1)}, u32[]{:S(2)}, u32[]{:S(2)}) %all-to-all-start.2) | async-done | bytes 1048608 | tf_op jit(solution)/shard_map/all_to_all | solution.py:158
  64.1 0.0 copy-start.4
  64.1 1.0 copy-done.4
  65.1 5.1 %all-to-all-start.1 = ((bf16[2,32,8,1024]{3,2,0,1:T(8,128)(2,1)}), bf16[2,32,8,1024]{3,2,0,1:T(8,128)(2,1)S(1)}, u32[]{:S(2)}, u32[]{:S(2)}) async-start(bf16[2,32,8,1024]{3,2,0,1:T(8,128)(2,1)} %copy.42), calls=%async_computation.1 | async-start | bytes 2097152 | tf_op jit(solution)/shard_map/all_to_all | solution.py:149
  70.1 0.0 copy-start.10
  70.1 0.0 copy-start.11
  70.1 2.6 %fusion.3 = f32[2,256,384]{2,1,0:T(8,128)S(1)} fusion(bf16[2,384,1024]{2,1,0:T(8,128)(2,1)} %param.12, bf16[2,32,8,1024]{3,2,0,1:T(8,128)(2,1)} %copy-done.4), kind=kOutput, calls=%fused_computation.15 | convolution fusion | flops 402653184 | bytes 3407872 | tf_op jit(solution)/shard_map/erd,ehd->erh/dot_general | solution.py:160
  72.7 0.0 copy-done.10
  72.8 0.0 copy-done.11
  72.8 0.8 fusion.18
  73.6 0.8 fusion.1
  74.4 1.1 copy.47
  75.5 0.0 copy-start.7
  75.5 10.8 %all-to-all-done.1 = bf16[2,32,8,1024]{3,2,0,1:T(8,128)(2,1)S(1)} async-done(((bf16[2,32,8,1024]{3,2,0,1:T(8,128)(2,1)}), bf16[2,32,8,1024]{3,2,0,1:T(8,128)(2,1)S(1)}, u32[]{:S(2)}, u32[]{:S(2)}) %all-to-all-start.1) | async-done | bytes 1048608 | tf_op jit(solution)/shard_map/all_to_all | solution.py:149
  86.3 0.0 copy-start.1
  86.3 5.7 %all-to-all-start.3 = ((bf16[2,32,8,1024]{3,2,0,1:T(8,128)(2,1)}), bf16[2,32,8,1024]{3,2,0,1:T(8,128)(2,1)}, u32[]{:S(2)}, u32[]{:S(2)}) async-start(bf16[2,32,8,1024]{3,2,0,1:T(8,128)(2,1)} %copy.47), calls=%async_computation.3 | async-start | bytes 2097152 | tf_op jit(solution)/shard_map/all_to_all | solution.py:181
  92.1 0.0 copy-start.5
  92.1 0.0 copy-done.7
  92.1 1.6 convolution_convert_fusion.1
  93.7 0.0 copy-done.1
  93.7 0.0 copy-done.5
  93.7 0.5 convolution_convert_fusion.2
  94.2 0.1 pad_maximum_fusion.refs_0_
  94.3 0.0 copy-start.2
  94.3 60.2 %shard_map.94 = f32[2,32,384]{2,1,0:T(8,128)S(1)} custom-call(bf16[1024,768]{1,0:T(8,128)(2,1)S(1)} %pad_maximum_fusion.refs_0_), custom_call_target="tpu_custom_call" | custom-call | tf_op jit(solution)/shard_map/pallas_call | solution.py:103
  154.5 0.0 copy-done.2
  154.6 0.1 copy.43
  154.6 1.2 gather_fusion
  155.8 1.0 fusion.2
  156.8 0.0 all-to-all-done.3
  156.8 1.3 copy.48
  158.1 1.2 gather_fusion.1
  159.3 1.0 bitcast_reduce_fusion
  160.3 0.6 copy.70
  (8 shorter events, 0.1 us)
Async XLA Ops:
  0.6 49.7 %copy-start = (bf16[2,1024,384]{2,1,0:T(8,128)(2,1)S(1)}, bf16[2,1024,384]{2,1,0:T(8,128)(2,1)}, u32[]{:S(2)}) copy-start(bf16[2,1024,384]{2,1,0:T(8,128)(2,1)} %param.11) | copy-start | bytes 4718596
  7.9 18.7 %copy-start.9 = (f32[32,8]{0,1:T(8,128)S(1)}, f32[32,8]{0,1:T(8,128)}, u32[]{:S(2)}) copy-start(f32[32,8]{0,1:T(8,128)} %param.9) | copy-start | bytes 3076
  9.0 17.7 %copy-start.8 = (bf16[32,1024]{1,0:T(8,128)(2,1)S(1)}, bf16[32,1024]{1,0:T(8,128)(2,1)}, u32[]{:S(2)}) copy-start(bf16[32,1024]{1,0:T(8,128)(2,1)} %param.13) | copy-start | bytes 196612
  9.0 33.8 %all-to-all-start = ((bf16[2,32,8,1024]{3,2,0,1:T(8,128)(2,1)}), bf16[2,32,8,1024]{3,2,0,1:T(8,128)(2,1)}, u32[]{:S(2)}, u32[]{:S(2)}) async-start(bf16[2,32,8,1024]{3,2,0,1:T(8,128)(2,1)} %copy.40), calls=%async_computation | async-start | bytes 2097152 | tf_op jit(solution)/shard_map/all_to_all | solution.py:139
  42.8 21.3 %all-to-all-start.2 = ((bf16[2,32,8,1024]{3,2,0,1:T(8,128)(2,1)}), bf16[2,32,8,1024]{3,2,0,1:T(8,128)(2,1)S(1)}, u32[]{:S(2)}, u32[]{:S(2)}) async-start(bf16[2,32,8,1024]{3,2,0,1:T(8,128)(2,1)} %copy.45), calls=%async_computation.2 | async-start | bytes 2097152 | tf_op jit(solution)/shard_map/all_to_all | solution.py:158
  50.3 3.0 %copy-start.3 = (bf16[2,384,1024]{2,1,0:T(8,128)(2,1)S(1)}, bf16[2,384,1024]{2,1,0:T(8,128)(2,1)}, u32[]{:S(2)}) copy-start(bf16[2,384,1024]{2,1,0:T(8,128)(2,1)} %param.12) | copy-start | bytes 4718596
  53.3 0.8 copy-start.6
  64.1 1.0 copy-start.4
  65.1 21.3 %all-to-all-start.1 = ((bf16[2,32,8,1024]{3,2,0,1:T(8,128)(2,1)}), bf16[2,32,8,1024]{3,2,0,1:T(8,128)(2,1)S(1)}, u32[]{:S(2)}, u32[]{:S(2)}) async-start(bf16[2,32,8,1024]{3,2,0,1:T(8,128)(2,1)} %copy.42), calls=%async_computation.1 | async-start | bytes 2097152 | tf_op jit(solution)/shard_map/all_to_all | solution.py:149
  70.1 2.6 %copy-start.10 = (bf16[2,1024,384]{2,1,0:T(8,128)(2,1)S(1)}, bf16[2,1024,384]{2,1,0:T(8,128)(2,1)}, u32[]{:S(2)}) copy-start(bf16[2,1024,384]{2,1,0:T(8,128)(2,1)} %param.10) | copy-start | bytes 4718596
  70.1 2.6 %copy-start.11 = (f32[2,256,384]{2,1,0:T(8,128)S(1)}, f32[2,256,384]{2,1,0:T(8,128)}, u32[]{:S(2)}) copy-start(f32[2,256,384]{2,1,0:T(8,128)} %get-tuple-element.4) | copy-start | bytes 2359300
  75.5 16.6 %copy-start.7 = (bf16[2,256,384]{2,1,0:T(8,128)(2,1)S(1)}, bf16[2,256,384]{2,1,0:T(8,128)(2,1)}, u32[]{:S(2)}) copy-start(bf16[2,256,384]{2,1,0:T(8,128)(2,1)} %copy-done.6) | copy-start | bytes 1179652
  86.3 7.3 %copy-start.1 = (bf16[2,32,8,1024]{3,2,0,1:T(8,128)(2,1)}, bf16[2,32,8,1024]{3,2,0,1:T(8,128)(2,1)S(1)}, u32[]{:S(2)}) copy-start(bf16[2,32,8,1024]{3,2,0,1:T(8,128)(2,1)S(1)} %all-to-all-done.1) | copy-start | bytes 3145732
  86.3 70.5 %all-to-all-start.3 = ((bf16[2,32,8,1024]{3,2,0,1:T(8,128)(2,1)}), bf16[2,32,8,1024]{3,2,0,1:T(8,128)(2,1)}, u32[]{:S(2)}, u32[]{:S(2)}) async-start(bf16[2,32,8,1024]{3,2,0,1:T(8,128)(2,1)} %copy.47), calls=%async_computation.3 | async-start | bytes 2097152 | tf_op jit(solution)/shard_map/all_to_all | solution.py:181
  92.1 1.6 %copy-start.5 = (bf16[2,32,8,1024]{3,2,0,1:T(8,128)(2,1)S(1)}, bf16[2,32,8,1024]{3,2,0,1:T(8,128)(2,1)}, u32[]{:S(2)}) copy-start(bf16[2,32,8,1024]{3,2,0,1:T(8,128)(2,1)} %copy-done.4) | copy-start | bytes 3145732
  94.3 60.2 %copy-start.2 = (bf16[2,32,8,1024]{3,2,0,1:T(8,128)(2,1)S(1)}, bf16[2,32,8,1024]{3,2,0,1:T(8,128)(2,1)}, u32[]{:S(2)}) copy-start(bf16[2,32,8,1024]{3,2,0,1:T(8,128)(2,1)} %copy-done.1) | copy-start | bytes 3145732

commit v2 on v0

v2 whole, which is shorter than its diff:
```python
import jax
import jax.numpy as jnp
from jax import lax
from jax.experimental import pallas as pl
from jax.experimental.pallas import tpu as pltpu
from jax.sharding import PartitionSpec as P

MESH = pl.DeviceIdType.MESH
F32 = jnp.float32
BF16 = jnp.bfloat16
SIDE = 4
CHIPS = SIDE * SIDE
TILE = 256

PARENT = {1: 2, 2: 3, 3: 0, 4: 3, 5: 4, 6: 7, 7: 8, 8: 3, 9: 8, 10: 9, 11: 12, 12: 13, 13: 8, 14: 13, 15: 14, 16: 14}
NEXT = dict(PARENT)
NEXT.update({-far: -near for far, near in PARENT.items() if far < 16})
FROM = {near: [far for far in NEXT if NEXT[far] == near] for near in set(NEXT.values())}
LEAVES = [far for far in (16, 15, -15, 11, -11, 10, -10, 6, -6, 5, -5, 1, -1)]


def dot(a, b):
    return lax.dot_general(a, b, (((1,), (0,)), ((), ())), preferred_element_type=F32)


def dot_nt(a, b):
    return lax.dot_general(a, b, (((1,), (1,)), ((), ())), preferred_element_type=F32)


def dot_tn(a, b):
    return lax.dot_general(a, b, (((0,), (0,)), ((), ())), preferred_element_type=F32)


def layer_kernel(
    n_dp,
    tok_hbm, ids_hbm, prob_hbm, wg_hbm, wu_hbm, wd_hbm, grad_hbm,
    mixed_ref, tgrad_ref, down_ref,
    ids_ref, prob_ref, x_all, dy_all, wg, wu, wd, coef_g, coef_u, ph, con_m, con_t, pair_m, pair_t, row_m, row_t, col_m, col_t, part, ring,
    own_sem, w_sem, ag_send, ag_recv, in_send, in_recv, pair_send, pair_recv, row_send, row_recv, col_send, col_recv, z_send, z_recv,
):
    e = lax.axis_index("expert")
    z = lax.axis_index("dp")
    rows, width = tok_hbm.shape
    half = CHIPS * rows
    hid = wg_hbm.shape[2]
    share = width // n_dp
    c = lax.rem(e, 2)
    x = lax.rem(lax.div(e, 2), SIDE)
    y = lax.div(e, 2 * SIDE)
    p = x + c * (y - x)
    q = y + c * (x - y)
    other = e + 1 - 2 * c

    def peer(dp, dq):
        p2, q2 = lax.rem(p + dp, SIDE), lax.rem(q + dq, SIDE)
        x2, y2 = p2 + c * (q2 - p2), q2 + c * (p2 - q2)
        return (y2 * SIDE + x2) * 2 + c

    def block(rp, rq):
        slot = lax.rem(q + SIDE - rq, SIDE) * SIDE + lax.rem(p + SIDE - rp, SIDE)
        return pl.multiple_of(slot * rows, rows)

    mine = block(0, 0)
    own = [
        pltpu.make_async_copy(ids_hbm, ids_ref, own_sem.at[0]),
        pltpu.make_async_copy(prob_hbm, prob_ref, own_sem.at[1]),
        pltpu.make_async_copy(tok_hbm, x_all.at[pl.ds(mine, rows), :width], own_sem.at[2]),
        pltpu.make_async_copy(grad_hbm, dy_all.at[pl.ds(mine, rows), :], own_sem.at[3]),
    ]
    for load in own:
        load.start()

    loads = []
    for k, (src, dst) in enumerate(((wg_hbm, wg), (wu_hbm, wu), (wd_hbm, wd))):
        for i in range(2):
            place = dst.at[i * hid : (i + 1) * hid, :] if k == 2 else dst.at[:, i * hid : (i + 1) * hid]
            load = pltpu.make_async_copy(src.at[i], place, w_sem.at[k, i])
            load.start()
            loads.append(load)

    barrier = pltpu.get_barrier_semaphore()
    near = [{"expert": other}]
    for r in range(1, SIDE):
        near.append({"expert": peer(r, 0)})
        near.append({"expert": peer(0, r)})
    reach = sorted({NEXT[far] - far for far in NEXT})
    for r in reach:
        near.append({"dp": lax.rem(z + n_dp - r, n_dp)})
    for device in near:
        pl.semaphore_signal(barrier, inc=1, device_id=device, device_id_type=MESH)

    experts = x_all.shape[1] - width
    experts //= 2
    expert_of = lax.broadcasted_iota(jnp.int32, (experts, rows), 0)
    gates = jnp.zeros((experts, rows), F32)
    own[0].wait()
    own[1].wait()
    for k in range(ids_ref.shape[0]):
        gates = gates + jnp.where(ids_ref[k : k + 1, :] == expert_of, prob_ref[k : k + 1, :], 0.0)
    high = gates.astype(BF16)
    low = (gates - high.astype(F32)).astype(BF16)
    line = lax.broadcasted_iota(jnp.int32, (experts, 2 * experts), 0)
    lane = lax.broadcasted_iota(jnp.int32, (experts, 2 * experts), 1)
    spread = dot_tn(high, (line == lane).astype(BF16)) + dot_tn(low, (line + experts == lane).astype(BF16))
    x_all[pl.ds(mine, rows), width:] = spread.astype(BF16)
    own[2].wait()
    own[3].wait()

    arrays = (x_all, dy_all)

    def gather(t, rp, rq):
        at = block(0, 0) if rq == 0 else block(rp, 0)
        ref = arrays[t].at[pl.ds(at, rows), :]
        return pltpu.make_async_remote_copy(
            src_ref=ref,
            dst_ref=ref,
            send_sem=ag_send.at[t, rp, rq],
            recv_sem=ag_recv.at[t, rp, rq],
            device_id={"expert": peer(rp, 0) if rq == 0 else peer(0, rq)},
            device_id_type=MESH,
        )

    def cross(t, rp, rq):
        at = block(rp, rq)
        return pltpu.make_async_remote_copy(
            src_ref=arrays[t].at[pl.ds(at, rows), :],
            dst_ref=arrays[t].at[pl.ds(pl.multiple_of(half + at, rows), rows), :],
            send_sem=in_send.at[t, rp, rq],
            recv_sem=in_recv.at[t, rp, rq],
            device_id={"expert": other},
            device_id_type=MESH,
        )

    pl.semaphore_wait(barrier, len(near))

    for t in range(2):
        for r in range(1, SIDE):
            gather(t, r, 0).start()
        for r in range(1, SIDE):
            gather(t, 0, r).start()
        cross(t, 0, 0).start()
    for t in range(2):
        for rp in (1, 3, 2):
            gather(t, rp, 0).wait_recv()
            for rq in range(1, SIDE):
                gather(t, rp, rq).start()
            cross(t, rp, 0).start()

    def pass_on(t):
        for rp in range(SIDE):
            for rq in range(1, SIDE):
                gather(t, rp, rq).wait_recv()
                cross(t, rp, rq).start()

    row_of = lax.broadcasted_iota(jnp.int32, (2 * experts, 2 * hid), 0)
    row_of = jnp.where(row_of >= experts, row_of - experts, row_of)
    col_of = lax.broadcasted_iota(jnp.int32, (2 * experts, 2 * hid), 1)
    pick = (row_of == jnp.where(col_of >= hid, 2 * e + 1, 2 * e)).astype(BF16)

    def forward(i, carry):
        at = pl.ds(pl.multiple_of(i * TILE, TILE), TILE)
        gate = dot(x_all[at, :width], wg[...])
        up = dot(x_all[at, :width], wu[...])
        prob = dot(x_all[at, width:], pick)
        sig = jax.nn.sigmoid(gate)
        act = gate * sig
        scaled = prob * act
        ph[at, :] = (scaled * up).astype(BF16)
        coef_u[at, :] = scaled
        coef_g[at, :] = prob * up * sig * (1.0 + gate * (1.0 - sig))
        return carry

    tiles = half // TILE
    pass_on(0)
    for load in loads[:4]:
        load.wait()
    lax.fori_loop(0, tiles, forward, 0)
    pass_on(1)
    for rp in range(SIDE):
        for rq in range(SIDE):
            cross(0, rp, rq).wait_recv()
    lax.fori_loop(tiles, 2 * tiles, forward, 0)
    for rp in range(SIDE):
        for rq in range(SIDE):
            cross(1, rp, rq).wait_recv()

    def partial(i, carry):
        at = pl.ds(pl.multiple_of(i * 128, 128), 128)
        part[at, :] = dot_tn(dy_all[:, at], ph[...]).astype(BF16)
        return carry

    lax.fori_loop(0, width // 128, partial, 0)

    def owned(far):
        owner = lax.rem(z + n_dp - far, n_dp)
        return pl.ds(pl.multiple_of(owner * share, share), share)

    def travel(far):
        src = ring.at[slot_of[FROM[far][0]]] if far in FROM else part.at[owned(far), :]
        return pltpu.make_async_remote_copy(
            src_ref=src,
            dst_ref=ring.at[slot_of[far]],
            send_sem=z_send.at[slot_of[far]],
            recv_sem=z_recv.at[slot_of[far]],
            device_id={"dp": lax.rem(z + n_dp + NEXT[far] - far, n_dp)},
            device_id_type=MESH,
        )

    slot_of = {far: k for k, far in enumerate(sorted(NEXT))}

    def add_up(far):
        total = part[owned(far), :].astype(F32)
        for child in FROM[far]:
            travel(child).wait_recv()
            total = total + ring[slot_of[child]].astype(F32)
        return total

    def relay(*fars):
        for far in fars:
            ring[slot_of[FROM[far][0]]] = add_up(far).astype(BF16)
            travel(far).start()

    for far in LEAVES:
        travel(far).start()

    def outputs(i, carry):
        at = pl.ds(pl.multiple_of(i * TILE, TILE), TILE)
        con_m[at, :] = dot(ph[at, :], wd[...]).astype(BF16)
        return carry

    def backward(i, carry):
        at = pl.ds(pl.multiple_of(i * TILE, TILE), TILE)
        hidden_grad = dot_nt(dy_all[at, :], wd[...])
        gate_grad = (hidden_grad * coef_g[at, :]).astype(BF16)
        up_grad = (hidden_grad * coef_u[at, :]).astype(BF16)
        con_t[at, :] = (dot_nt(gate_grad, wg[...]) + dot_nt(up_grad, wu[...])).astype(BF16)
        return carry

    sums = ((con_m, pair_m, row_m, col_m, mixed_ref), (con_t, pair_t, row_t, col_t, tgrad_ref))

    def pair(t):
        con, pairs = sums[t][:2]
        return pltpu.make_async_remote_copy(
            src_ref=con.at[half : 2 * half, :],
            dst_ref=pairs,
            send_sem=pair_send.at[t],
            recv_sem=pair_recv.at[t],
            device_id={"expert": other},
            device_id_type=MESH,
        )

    def line_at(rq):
        return pl.ds(pl.multiple_of(lax.rem(q + rq, SIDE) * (SIDE * rows), SIDE * rows), SIDE * rows)

    def to_line(t, r):
        con, _, lines = sums[t][:3]
        return pltpu.make_async_remote_copy(
            src_ref=con.at[line_at(r), :],
            dst_ref=lines.at[r - 1],
            send_sem=row_send.at[t, r - 1],
            recv_sem=row_recv.at[t, r - 1],
            device_id={"expert": peer(0, r)},
            device_id_type=MESH,
        )

    def send_lines(t):
        con, pairs = sums[t][:2]
        pair(t).wait_recv()
        for r in (2, 1, 3):
            at = line_at(r)
            con[at, :] = (con[at, :].astype(F32) + pairs[at, :].astype(F32)).astype(BF16)
            to_line(t, r).start()

    def block_at(r):
        return pl.multiple_of(lax.rem(q, SIDE) * (SIDE * rows) + lax.rem(p + r, SIDE) * rows, rows)

    def to_block(t, r):
        con, columns = sums[t][0], sums[t][3]
        return pltpu.make_async_remote_copy(
            src_ref=con.at[pl.ds(block_at(r), rows), :],
            dst_ref=columns.at[r - 1],
            send_sem=col_send.at[t, r - 1],
            recv_sem=col_recv.at[t, r - 1],
            device_id={"expert": peer(r, 0)},
            device_id_type=MESH,
        )

    def line_sum(t, r):
        con, pairs, lines = sums[t][:3]
        at = pl.ds(block_at(r), rows)
        inner = pl.ds(pl.multiple_of(lax.rem(p + r, SIDE) * rows, rows), rows)
        total = con[at, :].astype(F32) + pairs[at, :].astype(F32)
        for k in range(SIDE - 1):
            total = total + lines[k, inner, :].astype(F32)
        return total

    def send_blocks(t):
        con = sums[t][0]
        for r in range(1, SIDE):
            to_line(t, r).wait_recv()
        for r in (2, 1, 3):
            con[pl.ds(block_at(r), rows), :] = line_sum(t, r).astype(BF16)
            to_block(t, r).start()

    def finish(t):
        columns, out = sums[t][3:]
        total = line_sum(t, 0)
        for r in range(1, SIDE):
            to_block(t, r).wait_recv()
            total = total + columns[r - 1].astype(F32)
        out[...] = total.astype(BF16)

    for load in loads[4:]:
        load.wait()
    lax.fori_loop(tiles, 2 * tiles, outputs, 0)
    pair(0).start()
    lax.fori_loop(0, tiles, outputs, 0)
    relay(14, -14, 12, -12)
    relay(9, -9, 7, -7, 4, -4, 2, -2)
    lax.fori_loop(tiles, 2 * tiles, backward, 0)
    pair(1).start()
    relay(13, -13)
    send_lines(0)
    lax.fori_loop(0, tiles, backward, 0)
    relay(8, -8)
    send_lines(1)
    send_blocks(0)
    relay(3, -3)
    send_blocks(1)
    finish(0)
    finish(1)
    total = add_up(0)
    for i in range(2):
        down_ref[i] = total[:, i * hid : (i + 1) * hid]

    for t in range(2):
        for rp in range(SIDE):
            for rq in range(SIDE):
                cross(t, rp, rq).wait_send()
                if rp or rq:
                    gather(t, rp, rq).wait_send()
        pair(t).wait_send()
        for r in range(1, SIDE):
            to_line(t, r).wait_send()
            to_block(t, r).wait_send()
    for far in NEXT:
        travel(far).wait_send()


def on_device(n_dp, experts, tokens, expert_ids, gate_probs, w_gate, w_up, w_down, out_grad):
    rows, width = tokens.shape
    mine, _, hid = w_gate.shape
    half = CHIPS * rows
    share = width // n_dp
    vmem = pl.BlockSpec(memory_space=pltpu.VMEM)
    hbm = pl.BlockSpec(memory_space=pl.ANY)
    dma = pltpu.SemaphoreType.DMA
    reach = SIDE - 1
    mixed, token_grad, down = pl.pallas_call(
        lambda *refs: layer_kernel(n_dp, *refs),
        out_shape=(
            jax.ShapeDtypeStruct((rows, width), BF16),
            jax.ShapeDtypeStruct((rows, width), BF16),
            jax.ShapeDtypeStruct((mine, share, hid), F32),
        ),
        in_specs=[hbm] * 7,
        out_specs=(vmem, vmem, vmem),
        scratch_shapes=[
            pltpu.VMEM(expert_ids.shape[::-1], jnp.int32),
            pltpu.VMEM(gate_probs.shape[::-1], F32),
            pltpu.VMEM((2 * half, width + 2 * experts), BF16),
            pltpu.VMEM((2 * half, width), BF16),
            pltpu.VMEM((width, mine * hid), BF16),
            pltpu.VMEM((width, mine * hid), BF16),
            pltpu.VMEM((mine * hid, width), BF16),
            pltpu.VMEM((2 * half, mine * hid), F32),
            pltpu.VMEM((2 * half, mine * hid), F32),
            pltpu.VMEM((2 * half, mine * hid), BF16),
            pltpu.VMEM((2 * half, width), BF16),
            pltpu.VMEM((2 * half, width), BF16),
            pltpu.VMEM((half, width), BF16),
            pltpu.VMEM((half, width), BF16),
            pltpu.VMEM((reach, SIDE * rows, width), BF16),
            pltpu.VMEM((reach, SIDE * rows, width), BF16),
            pltpu.VMEM((reach, rows, width), BF16),
            pltpu.VMEM((reach, rows, width), BF16),
            pltpu.VMEM((width, mine * hid), BF16),
            pltpu.VMEM((len(NEXT), share, mine * hid), BF16),
            dma((4,)),
            dma((3, 2)),
            dma((2, SIDE, SIDE)),
            dma((2, SIDE, SIDE)),
            dma((2, SIDE, SIDE)),
            dma((2, SIDE, SIDE)),
            dma((2,)),
            dma((2,)),
            dma((2, reach)),
            dma((2, reach)),
            dma((2, reach)),
            dma((2, reach)),
            dma((len(NEXT),)),
            dma((len(NEXT),)),
        ],
        compiler_params=pltpu.CompilerParams(
            collective_id=0, has_side_effects=True, vmem_limit_bytes=58 * 1024 * 1024
        ),
    )(tokens, expert_ids.T, gate_probs.T, w_gate, w_up, w_down, out_grad)
    return mixed, token_grad, jnp.transpose(down, (0, 2, 1))


def solution(mesh):
    n_dp = mesh.shape["dp"]

    def body(*args):
        return on_device(n_dp, args[3].shape[0] * mesh.shape["expert"], *args)

    return jax.shard_map(
        body,
        mesh=mesh,
        in_specs=(
            P(("expert", "dp"), None),
            P(("expert", "dp"), None),
            P(("expert", "dp"), None),
            P("expert", None, None),
            P("expert", None, None),
            P("expert", None, None),
            P(("expert", "dp"), None),
        ),
        out_specs=(P(("expert", "dp"), None), P(("expert", "dp"), None), P("expert", None, "dp")),
        check_vma=False,
    )
```

time: 284 us -> 94.6 us (0.33)
  the two profiles are of different devices: /device:TPU:14 before, /device:TPU:2 now
where the time goes in v2:
time: 94.6 us; the launch traced here: 94.4 us
  Pallas kernels  89.2 us (94%)
  local copies, waits for them, and re-layouts  4.48 us (5%)
    pallas_call x1, Pallas kernels, on_device(): pl.pallas_call(lambda *refs: layer_kernel(n_dp, *refs), out_shape=(jax.Sh...  89.2 us
    unnamed x3, local copies, waits for them, and re-layouts  4.48 us

profile of v2, /device:TPU:2, one launch (start us, length us, event | category | flops | bytes accessed | tf_op | source)
XLA Modules:
  0.0 94.4 jit_solution(11177038983148135292)
XLA Ops:
  0.6 89.2 %shard_map.94 = (bf16[32,1024]{1,0:T(8,128)(2,1)}, bf16[32,1024]{1,0:T(8,128)(2,1)}, f32[2,32,384]{2,1,0:T(8,128)}) custom-call(bf16[32,1024]{1,0:T(8,128)(2,1)} %refs_0_.1, s32[8,32]{1,0:T(8,128)} %bitcast.4, f32[8,32]{1,0:T(8,128)} %bitcast.5, bf16[2,1024,384]{2,1,0:T(8,128)(2,1)} %refs_3_.1, bf16[2,1024,384]{2,1,0:T(8,128)(2,1)} %refs_4_.1, ...), custom_call_target="tpu_custom_call" | custom-call | tf_op jit(solution)/shard_map/pallas_call | solution.py:359
  89.9 1.5 %copy.13 = bf16[32,1024]{1,0:T(8,128)(2,1)} copy(bf16[32,1024]{1,0:T(8,128)(2,1)} %get-tuple-element.12) | data formatting | bytes 131072
  91.4 1.5 %copy.14 = bf16[32,1024]{1,0:T(8,128)(2,1)} copy(bf16[32,1024]{1,0:T(8,128)(2,1)} %get-tuple-element.13) | data formatting | bytes 131072
  92.8 1.5 %copy.15 = f32[2,384,32]{1,2,0:T(8,128)} copy(f32[2,384,32]{1,2,0:T(8,128)} %bitcast.3) | data formatting | bytes 196608

commit v3 on v2

--- a/solution.py
+++ b/solution.py
@@ -11,12 +11,12 @@
 SIDE = 4
 CHIPS = SIDE * SIDE
 TILE = 256
+CAP = 8
 
 PARENT = {1: 2, 2: 3, 3: 0, 4: 3, 5: 4, 6: 7, 7: 8, 8: 3, 9: 8, 10: 9, 11: 12, 12: 13, 13: 8, 14: 13, 15: 14, 16: 14}
 NEXT = dict(PARENT)
 NEXT.update({-far: -near for far, near in PARENT.items() if far < 16})
 FROM = {near: [far for far in NEXT if NEXT[far] == near] for near in set(NEXT.values())}
-LEAVES = [far for far in (16, 15, -15, 11, -11, 10, -10, 6, -6, 5, -5, 1, -1)]
 
 
 def dot(a, b):
@@ -35,7 +35,7 @@
     n_dp,
     tok_hbm, ids_hbm, prob_hbm, wg_hbm, wu_hbm, wd_hbm, grad_hbm,
     mixed_ref, tgrad_ref, down_ref,
-    ids_ref, prob_ref, x_all, dy_all, wg, wu, wd, coef_g, coef_u, ph, con_m, con_t, pair_m, pair_t, row_m, row_t, col_m, col_t, part, ring,
+    ids_ref, prob_ref, x_all, dy_all, wg, wu, wd, slots, xs, dys, coef_g, coef_u, ph, outs, back, con_m, con_t, pair_m, pair_t, row_m, row_t, col_m, col_t, part, ring,
     own_sem, w_sem, ag_send, ag_recv, in_send, in_recv, pair_send, pair_recv, row_send, row_recv, col_send, col_recv, z_send, z_recv,
 ):
     e = lax.axis_index("expert")
@@ -72,11 +72,9 @@
 
     loads = []
     for k, (src, dst) in enumerate(((wg_hbm, wg), (wu_hbm, wu), (wd_hbm, wd))):
-        for i in range(2):
-            place = dst.at[i * hid : (i + 1) * hid, :] if k == 2 else dst.at[:, i * hid : (i + 1) * hid]
-            load = pltpu.make_async_copy(src.at[i], place, w_sem.at[k, i])
-            load.start()
-            loads.append(load)
+        load = pltpu.make_async_copy(src, dst, w_sem.at[k])
+        load.start()
+        loads.append(load)
 
     barrier = pltpu.get_barrier_semaphore()
     near = [{"expert": other}]
@@ -89,20 +87,29 @@
     for device in near:
         pl.semaphore_signal(barrier, inc=1, device_id=device, device_id_type=MESH)
 
-    experts = x_all.shape[1] - width
-    experts //= 2
+    lanes = 128
+    experts = 64
+    gate_at, code_at = width, width + lanes
     expert_of = lax.broadcasted_iota(jnp.int32, (experts, rows), 0)
-    gates = jnp.zeros((experts, rows), F32)
     own[0].wait()
     own[1].wait()
+    gates = jnp.zeros((experts, rows), F32)
+    taken = jnp.zeros((experts, rows), F32)
     for k in range(ids_ref.shape[0]):
-        gates = gates + jnp.where(ids_ref[k : k + 1, :] == expert_of, prob_ref[k : k + 1, :], 0.0)
+        hit = ids_ref[k : k + 1, :] == expert_of
+        gates = gates + jnp.where(hit, prob_ref[k : k + 1, :], 0.0)
+        taken = taken + jnp.where(hit, 1.0, 0.0)
     high = gates.astype(BF16)
     low = (gates - high.astype(F32)).astype(BF16)
-    line = lax.broadcasted_iota(jnp.int32, (experts, 2 * experts), 0)
-    lane = lax.broadcasted_iota(jnp.int32, (experts, 2 * experts), 1)
-    spread = dot_tn(high, (line == lane).astype(BF16)) + dot_tn(low, (line + experts == lane).astype(BF16))
-    x_all[pl.ds(mine, rows), width:] = spread.astype(BF16)
+    before = lax.broadcasted_iota(jnp.int32, (rows, rows), 0) < lax.broadcasted_iota(jnp.int32, (rows, rows), 1)
+    rank = dot(taken.astype(BF16), before.astype(F32).astype(BF16))
+    code = (taken * (rank + 1.0) - 1.0).astype(BF16)
+    line = lax.broadcasted_iota(jnp.int32, (experts, lanes), 0)
+    lane = lax.broadcasted_iota(jnp.int32, (experts, lanes), 1)
+    first = (line == lane).astype(F32).astype(BF16)
+    second = (line + experts == lane).astype(F32).astype(BF16)
+    x_all[pl.ds(mine, rows), gate_at:code_at] = (dot_tn(high, first) + dot_tn(low, second)).astype(BF16)
+    x_all[pl.ds(mine, rows), code_at:] = dot_tn(code, first).astype(BF16)
     own[2].wait()
     own[3].wait()
 
@@ -152,44 +159,76 @@
                 gather(t, rp, rq).wait_recv()
                 cross(t, rp, rq).start()
 
-    row_of = lax.broadcasted_iota(jnp.int32, (2 * experts, 2 * hid), 0)
-    row_of = jnp.where(row_of >= experts, row_of - experts, row_of)
-    col_of = lax.broadcasted_iota(jnp.int32, (2 * experts, 2 * hid), 1)
-    pick = (row_of == jnp.where(col_of >= hid, 2 * e + 1, 2 * e)).astype(BF16)
-
-    def forward(i, carry):
-        at = pl.ds(pl.multiple_of(i * TILE, TILE), TILE)
-        gate = dot(x_all[at, :width], wg[...])
-        up = dot(x_all[at, :width], wu[...])
-        prob = dot(x_all[at, width:], pick)
+    per = TILE // rows * CAP
+    line = lax.broadcasted_iota(jnp.int32, (lanes, 2 * per), 0)
+    lane = lax.broadcasted_iota(jnp.int32, (lanes, 2 * per), 1)
+    pick_code = (line == jnp.where(lane >= per, 2 * e + 1, 2 * e)).astype(F32).astype(BF16)
+    token = lax.broadcasted_iota(jnp.int32, (TILE, 2 * per), 0)
+    place = lax.broadcasted_iota(jnp.int32, (TILE, 2 * per), 1)
+    place = jnp.where(place >= per, place - per, place)
+    same = jnp.where((token >> 5) == (place >> 3), 1.0, 0.0)
+    wanted = (place & (CAP - 1)).astype(F32)
+
+    def tile_at(i):
+        return pl.ds(pl.multiple_of(i * TILE, TILE), TILE)
+
+    def rows_at(i):
+        return pl.ds(pl.multiple_of(i * per, per), per)
+
+    def pack_x(i, carry):
+        at = tile_at(i)
+        codes = dot(x_all[at, code_at:], pick_code)
+        chosen = (jnp.where(codes == wanted, 1.0, 0.0) * same).astype(BF16)
+        slots[at, :] = chosen
+        got = dot_tn(chosen, x_all[at, :code_at]).astype(BF16)
+        xs[0, rows_at(i), :] = got[:per]
+        xs[1, rows_at(i), :] = got[per:]
+        return carry
+
+    def pack_dy(i, carry):
+        got = dot_tn(slots[tile_at(i), :], dy_all[tile_at(i), :]).astype(BF16)
+        dys[0, rows_at(i), :] = got[:per]
+        dys[1, rows_at(i), :] = got[per:]
+        return carry
+
+    gate_line = lax.broadcasted_iota(jnp.int32, (lanes, hid), 0)
+    gate_line = jnp.where(gate_line >= experts, gate_line - experts, gate_line)
+
+    def forward(k, carry):
+        gate = dot(xs[k, :, :width], wg[k])
+        up = dot(xs[k, :, :width], wu[k])
+        prob = dot(xs[k, :, gate_at:], (gate_line == 2 * e + k).astype(F32).astype(BF16))
         sig = jax.nn.sigmoid(gate)
-        act = gate * sig
-        scaled = prob * act
-        ph[at, :] = (scaled * up).astype(BF16)
-        coef_u[at, :] = scaled
-        coef_g[at, :] = prob * up * sig * (1.0 + gate * (1.0 - sig))
+        scaled = prob * (gate * sig)
+        ph[k] = (scaled * up).astype(BF16)
+        coef_u[k] = scaled
+        coef_g[k] = prob * up * sig * (1.0 + gate * (1.0 - sig))
         return carry
 
     tiles = half // TILE
     pass_on(0)
-    for load in loads[:4]:
-        load.wait()
-    lax.fori_loop(0, tiles, forward, 0)
-    pass_on(1)
+    lax.fori_loop(0, tiles, pack_x, 0)
     for rp in range(SIDE):
         for rq in range(SIDE):
             cross(0, rp, rq).wait_recv()
-    lax.fori_loop(tiles, 2 * tiles, forward, 0)
+    lax.fori_loop(tiles, 2 * tiles, pack_x, 0)
+    pass_on(1)
+    for load in loads:
+        load.wait()
+    lax.fori_loop(0, 2, forward, 0)
+    lax.fori_loop(0, tiles, pack_dy, 0)
     for rp in range(SIDE):
         for rq in range(SIDE):
             cross(1, rp, rq).wait_recv()
+    lax.fori_loop(tiles, 2 * tiles, pack_dy, 0)
 
     def partial(i, carry):
-        at = pl.ds(pl.multiple_of(i * 128, 128), 128)
-        part[at, :] = dot_tn(dy_all[:, at], ph[...]).astype(BF16)
-        return carry
-
-    lax.fori_loop(0, width // 128, partial, 0)
+        at = tile_at(i)
+        for k in range(2):
+            part[at, k * hid : (k + 1) * hid] = dot_tn(dys[k, :, at], ph[k]).astype(BF16)
+        return carry
+
+    lax.fori_loop(0, width // TILE, partial, 0)
 
     def owned(far):
         owner = lax.rem(z + n_dp - far, n_dp)
@@ -220,34 +259,48 @@
             ring[slot_of[FROM[far][0]]] = add_up(far).astype(BF16)
             travel(far).start()
 
-    for far in LEAVES:
-        travel(far).start()
-
-    def outputs(i, carry):
-        at = pl.ds(pl.multiple_of(i * TILE, TILE), TILE)
-        con_m[at, :] = dot(ph[at, :], wd[...]).astype(BF16)
-        return carry
-
-    def backward(i, carry):
-        at = pl.ds(pl.multiple_of(i * TILE, TILE), TILE)
-        hidden_grad = dot_nt(dy_all[at, :], wd[...])
-        gate_grad = (hidden_grad * coef_g[at, :]).astype(BF16)
-        up_grad = (hidden_grad * coef_u[at, :]).astype(BF16)
-        con_t[at, :] = (dot_nt(gate_grad, wg[...]) + dot_nt(up_grad, wu[...])).astype(BF16)
-        return carry
+    def begin(*fars):
+        for far in fars:
+            travel(far).start()
+
+    begin(16, 15, -15, 11, -11)
+
+    def outputs(k, carry):
+        outs[k] = dot(ph[k], wd[k]).astype(BF16)
+        return carry
+
+    def backward(k, carry):
+        hidden_grad = dot_nt(dys[k], wd[k])
+        gate_grad = (hidden_grad * coef_g[k]).astype(BF16)
+        up_grad = (hidden_grad * coef_u[k]).astype(BF16)
+        back[k] = (dot_nt(gate_grad, wg[k]) + dot_nt(up_grad, wu[k])).astype(BF16)
+        return carry
+
+    def unpack(source, con):
+        def one(i, carry):
+            both = jnp.concatenate([source[0, rows_at(i), :], source[1, rows_at(i), :]], axis=0)
+            con[tile_at(i), :] = dot(slots[tile_at(i), :], both).astype(BF16)
+            return carry
+
+        return one
 
     sums = ((con_m, pair_m, row_m, col_m, mixed_ref), (con_t, pair_t, row_t, col_t, tgrad_ref))
 
-    def pair(t):
+    def pair(t, r):
         con, pairs = sums[t][:2]
-        return pltpu.make_async_remote_copy(
-            src_ref=con.at[half : 2 * half, :],
-            dst_ref=pairs,
-            send_sem=pair_send.at[t],
-            recv_sem=pair_recv.at[t],
+        at = lax.rem(p + r, SIDE) * (SIDE * rows)
+        return pltpu.make_async_remote_copy(
+            src_ref=con.at[pl.ds(pl.multiple_of(half + at, SIDE * rows), SIDE * rows), :],
+            dst_ref=pairs.at[pl.ds(pl.multiple_of(at, SIDE * rows), SIDE * rows), :],
+            send_sem=pair_send.at[t, r],
+            recv_sem=pair_recv.at[t, r],
             device_id={"expert": other},
             device_id_type=MESH,
         )
+
+    def send_pairs(t):
+        for r in (2, 1, 3, 0):
+            pair(t, r).start()
 
     def line_at(rq):
         return pl.ds(pl.multiple_of(lax.rem(q + rq, SIDE) * (SIDE * rows), SIDE * rows), SIDE * rows)
@@ -265,9 +318,9 @@
 
     def send_lines(t):
         con, pairs = sums[t][:2]
-        pair(t).wait_recv()
         for r in (2, 1, 3):
             at = line_at(r)
+            pair(t, r).wait_recv()
             con[at, :] = (con[at, :].astype(F32) + pairs[at, :].astype(F32)).astype(BF16)
             to_line(t, r).start()
 
@@ -296,6 +349,7 @@
 
     def send_blocks(t):
         con = sums[t][0]
+        pair(t, 0).wait_recv()
         for r in range(1, SIDE):
             to_line(t, r).wait_recv()
         for r in (2, 1, 3):
@@ -310,24 +364,27 @@
             total = total + columns[r - 1].astype(F32)
         out[...] = total.astype(BF16)
 
-    for load in loads[4:]:
-        load.wait()
-    lax.fori_loop(tiles, 2 * tiles, outputs, 0)
-    pair(0).start()
-    lax.fori_loop(0, tiles, outputs, 0)
+    lax.fori_loop(0, 2, outputs, 0)
+    lax.fori_loop(tiles, 2 * tiles, unpack(outs, con_m), 0)
+    send_pairs(0)
+    begin(10, -10, 6, -6)
+    lax.fori_loop(0, 2, backward, 0)
+    lax.fori_loop(tiles, 2 * tiles, unpack(back, con_t), 0)
+    send_pairs(1)
     relay(14, -14, 12, -12)
-    relay(9, -9, 7, -7, 4, -4, 2, -2)
-    lax.fori_loop(tiles, 2 * tiles, backward, 0)
-    pair(1).start()
+    begin(5, -5, 1, -1)
+    lax.fori_loop(0, tiles, unpack(outs, con_m), 0)
+    send_lines(0)
+    lax.fori_loop(0, tiles, unpack(back, con_t), 0)
     relay(13, -13)
-    send_lines(0)
-    lax.fori_loop(0, tiles, backward, 0)
+    relay(9, -9, 7, -7)
+    send_lines(1)
+    relay(4, -4, 2, -2)
+    send_blocks(0)
     relay(8, -8)
-    send_lines(1)
-    send_blocks(0)
-    relay(3, -3)
     send_blocks(1)
     finish(0)
+    relay(3, -3)
     finish(1)
     total = add_up(0)
     for i in range(2):
@@ -339,7 +396,8 @@
                 cross(t, rp, rq).wait_send()
                 if rp or rq:
                     gather(t, rp, rq).wait_send()
-        pair(t).wait_send()
+        for r in range(SIDE):
+            pair(t, r).wait_send()
         for r in range(1, SIDE):
             to_line(t, r).wait_send()
             to_block(t, r).wait_send()
@@ -347,13 +405,14 @@
         travel(far).wait_send()
 
 
-def on_device(n_dp, experts, tokens, expert_ids, gate_probs, w_gate, w_up, w_down, out_grad):
+def on_device(n_dp, tokens, expert_ids, gate_probs, w_gate, w_up, w_down, out_grad):
     rows, width = tokens.shape
     mine, _, hid = w_gate.shape
     half = CHIPS * rows
     share = width // n_dp
+    taken = 2 * CHIPS * CAP
     vmem = pl.BlockSpec(memory_space=pltpu.VMEM)
-    hbm = pl.BlockSpec(memory_space=pl.ANY)
+    hbm = pl.BlockSpec(memory_space=pltpu.HBM)
     dma = pltpu.SemaphoreType.DMA
     reach = SIDE - 1
     mixed, token_grad, down = pl.pallas_call(
@@ -368,14 +427,19 @@
         scratch_shapes=[
             pltpu.VMEM(expert_ids.shape[::-1], jnp.int32),
             pltpu.VMEM(gate_probs.shape[::-1], F32),
-            pltpu.VMEM((2 * half, width + 2 * experts), BF16),
+            pltpu.VMEM((2 * half, width + 256), BF16),
             pltpu.VMEM((2 * half, width), BF16),
-            pltpu.VMEM((width, mine * hid), BF16),
-            pltpu.VMEM((width, mine * hid), BF16),
-            pltpu.VMEM((mine * hid, width), BF16),
-            pltpu.VMEM((2 * half, mine * hid), F32),
-            pltpu.VMEM((2 * half, mine * hid), F32),
-            pltpu.VMEM((2 * half, mine * hid), BF16),
+            pltpu.VMEM((mine, width, hid), BF16),
+            pltpu.VMEM((mine, width, hid), BF16),
+            pltpu.VMEM((mine, hid, width), BF16),
+            pltpu.VMEM((2 * half, 2 * TILE // rows * CAP), BF16),
+            pltpu.VMEM((mine, taken, width + 128), BF16),
+            pltpu.VMEM((mine, taken, width), BF16),
+            pltpu.VMEM((mine, taken, hid), F32),
+            pltpu.VMEM((mine, taken, hid), F32),
+            pltpu.VMEM((mine, taken, hid), BF16),
+            pltpu.VMEM((mine, taken, width), BF16),
+            pltpu.VMEM((mine, taken, width), BF16),
             pltpu.VMEM((2 * half, width), BF16),
             pltpu.VMEM((2 * half, width), BF16),
             pltpu.VMEM((half, width), BF16),
@@ -387,13 +451,13 @@
             pltpu.VMEM((width, mine * hid), BF16),
             pltpu.VMEM((len(NEXT), share, mine * hid), BF16),
             dma((4,)),
-            dma((3, 2)),
+            dma((3,)),
             dma((2, SIDE, SIDE)),
             dma((2, SIDE, SIDE)),
             dma((2, SIDE, SIDE)),
             dma((2, SIDE, SIDE)),
-            dma((2,)),
-            dma((2,)),
+            dma((2, SIDE)),
+            dma((2, SIDE)),
             dma((2, reach)),
             dma((2, reach)),
             dma((2, reach)),
@@ -412,7 +476,7 @@
     n_dp = mesh.shape["dp"]
 
     def body(*args):
-        return on_device(n_dp, args[3].shape[0] * mesh.shape["expert"], *args)
+        return on_device(n_dp, *args)
 
     return jax.shard_map(
         body,

time: 94.6 us -> 88.6 us (0.937)
  the two profiles are of different devices: /device:TPU:2 before, /device:TPU:96 now
where the time goes in v3:
time: 88.6 us; the launch traced here: 88.3 us
  Pallas kernels  83.2 us (94%)
  local copies, waits for them, and re-layouts  4.48 us (5%)
    pallas_call x1, Pallas kernels, on_device(): pl.pallas_call(lambda *refs: layer_kernel(n_dp, *refs), out_shape=(jax.Sh...  83.2 us
    unnamed x3, local copies, waits for them, and re-layouts  4.48 us

profile of v3, /device:TPU:96, one launch (start us, length us, event | category | flops | bytes accessed | tf_op | source)
XLA Modules:
  0.0 88.3 jit_solution(146937036688181434)
XLA Ops:
  0.6 83.2 %shard_map.94 = (bf16[32,1024]{1,0:T(8,128)(2,1)}, bf16[32,1024]{1,0:T(8,128)(2,1)}, f32[2,32,384]{2,1,0:T(8,128)}) custom-call(bf16[32,1024]{1,0:T(8,128)(2,1)} %refs_0_.1, s32[8,32]{1,0:T(8,128)} %bitcast.4, f32[8,32]{1,0:T(8,128)} %bitcast.5, bf16[2,1024,384]{2,1,0:T(8,128)(2,1)} %refs_3_.1, bf16[2,1024,384]{2,1,0:T(8,128)(2,1)} %refs_4_.1, ...), custom_call_target="tpu_custom_call" | custom-call | tf_op jit(solution)/shard_map/pallas_call | solution.py:418
  83.8 1.5 %copy.13 = bf16[32,1024]{1,0:T(8,128)(2,1)} copy(bf16[32,1024]{1,0:T(8,128)(2,1)} %get-tuple-element.12) | data formatting | bytes 131072
  85.3 1.5 %copy.14 = bf16[32,1024]{1,0:T(8,128)(2,1)} copy(bf16[32,1024]{1,0:T(8,128)(2,1)} %get-tuple-element.13) | data formatting | bytes 131072
  86.7 1.5 %copy.15 = f32[2,384,32]{1,2,0:T(8,128)} copy(f32[2,384,32]{1,2,0:T(8,128)} %bitcast.3) | data formatting | bytes 196608

commit v4 on v3

--- a/solution.py
+++ b/solution.py
@@ -403,6 +403,12 @@
             to_block(t, r).wait_send()
     for far in NEXT:
         travel(far).wait_send()
+
+
+def hand_over(*refs):
+    n = len(refs) // 2
+    for k in range(n):
+        refs[n + k][...] = refs[k][...]
 
 
 def on_device(n_dp, tokens, expert_ids, gate_probs, w_gate, w_up, w_down, out_grad):
@@ -469,6 +475,14 @@
             collective_id=0, has_side_effects=True, vmem_limit_bytes=58 * 1024 * 1024
         ),
     )(tokens, expert_ids.T, gate_probs.T, w_gate, w_up, w_down, out_grad)
+    results = (mixed, token_grad, down)
+    mixed, token_grad, down = pl.pallas_call(
+        hand_over,
+        out_shape=tuple(jax.ShapeDtypeStruct(part.shape, part.dtype) for part in results),
+        in_specs=[vmem] * 3,
+        out_specs=(vmem,) * 3,
+        compiler_params=pltpu.CompilerParams(vmem_limit_bytes=58 * 1024 * 1024),
+    )(*results)
     return mixed, token_grad, jnp.transpose(down, (0, 2, 1))
 
 

time: 88.6 us -> 85.6 us (0.966)
  local copies, waits for them, and re-layouts: 4.48 us -> 0 us
  Pallas kernels: 83.2 us -> 84.8 us
    unnamed x3 -> x0, local copies, waits for them, and re-layouts: 4.48 us -> none
    pallas_call x0 -> x1, Pallas kernels: none -> 1.66 us  [on_device(): pl.pallas_call(hand_over, out_shape=tuple((jax.ShapeDtypeStruct(part.shap...]
where the time goes in v4:
time: 85.6 us; the launch traced here: 85.4 us
  Pallas kernels  84.8 us (99%)
    pallas_call x1, Pallas kernels, on_device(): pl.pallas_call(lambda *refs: layer_kernel(n_dp, *refs), out_shape=(jax.Sh...  83.1 us

profile of v4, /device:TPU:96, one launch (start us, length us, event | category | flops | bytes accessed | tf_op | source)
XLA Modules:
  0.0 85.4 jit_solution(16541463559225812914)
XLA Ops:
  0.6 83.1 %shard_map.94 = (bf16[32,1024]{1,0:T(8,128)(2,1)}, bf16[32,1024]{1,0:T(8,128)(2,1)}, f32[2,32,384]{2,1,0:T(8,128)}) custom-call(bf16[32,1024]{1,0:T(8,128)(2,1)} %refs_0_.1, s32[8,32]{1,0:T(8,128)} %bitcast.3, f32[8,32]{1,0:T(8,128)} %bitcast.4, bf16[2,1024,384]{2,1,0:T(8,128)(2,1)} %refs_3_.1, bf16[2,1024,384]{2,1,0:T(8,128)(2,1)} %refs_4_.1, ...), custom_call_target="tpu_custom_call" | custom-call | tf_op jit(solution)/shard_map/pallas_call | solution.py:424
  83.8 1.7 %shard_map.95 = (bf16[32,1024]{1,0:T(8,128)(2,1)}, bf16[32,1024]{1,0:T(8,128)(2,1)}, f32[2,32,384]{2,1,0:T(8,128)}) custom-call(bf16[32,1024]{1,0:T(8,128)(2,1)} %get-tuple-element.9.refs_0_, bf16[32,1024]{1,0:T(8,128)(2,1)} %get-tuple-element.10.refs_1_, f32[2,32,384]{2,1,0:T(8,128)} %get-tuple-element.11.refs_2_), custom_call_target="tpu_custom_call" | custom-call | tf_op jit(solution)/shard_map/pallas_call | solution.py:479

commit v5 on v4

--- a/solution.py
+++ b/solution.py
@@ -222,48 +222,53 @@
             cross(1, rp, rq).wait_recv()
     lax.fori_loop(tiles, 2 * tiles, pack_dy, 0)
 
-    def partial(i, carry):
-        at = tile_at(i)
-        for k in range(2):
-            part[at, k * hid : (k + 1) * hid] = dot_tn(dys[k, :, at], ph[k]).astype(BF16)
-        return carry
-
-    lax.fori_loop(0, width // TILE, partial, 0)
+    def partial(k):
+        def one(i, carry):
+            at = tile_at(i)
+            part[k, at, :] = dot_tn(dys[k, :, at], ph[k]).astype(BF16)
+            return carry
+
+        return one
+
+    slot_of = {far: k for k, far in enumerate(sorted(NEXT))}
 
     def owned(far):
         owner = lax.rem(z + n_dp - far, n_dp)
         return pl.ds(pl.multiple_of(owner * share, share), share)
 
-    def travel(far):
-        src = ring.at[slot_of[FROM[far][0]]] if far in FROM else part.at[owned(far), :]
+    def travel(far, k):
+        src = ring.at[slot_of[FROM[far][0]], k] if far in FROM else part.at[k, owned(far), :]
         return pltpu.make_async_remote_copy(
             src_ref=src,
-            dst_ref=ring.at[slot_of[far]],
-            send_sem=z_send.at[slot_of[far]],
-            recv_sem=z_recv.at[slot_of[far]],
+            dst_ref=ring.at[slot_of[far], k],
+            send_sem=z_send.at[slot_of[far], k],
+            recv_sem=z_recv.at[slot_of[far], k],
             device_id={"dp": lax.rem(z + n_dp + NEXT[far] - far, n_dp)},
             device_id_type=MESH,
         )
 
-    slot_of = {far: k for k, far in enumerate(sorted(NEXT))}
-
-    def add_up(far):
-        total = part[owned(far), :].astype(F32)
+    def add_up(far, k):
+        total = part[k, owned(far), :].astype(F32)
         for child in FROM[far]:
-            travel(child).wait_recv()
-            total = total + ring[slot_of[child]].astype(F32)
+            travel(child, k).wait_recv()
+            total = total + ring[slot_of[child], k, :, :].astype(F32)
         return total
 
     def relay(*fars):
-        for far in fars:
-            ring[slot_of[FROM[far][0]]] = add_up(far).astype(BF16)
-            travel(far).start()
+        for k in range(2):
+            for far in fars:
+                ring[slot_of[FROM[far][0]], k, :, :] = add_up(far, k).astype(BF16)
+                travel(far, k).start()
 
     def begin(*fars):
-        for far in fars:
-            travel(far).start()
-
-    begin(16, 15, -15, 11, -11)
+        for k in range(2):
+            for far in fars:
+                travel(far, k).start()
+
+    for k in range(2):
+        lax.fori_loop(0, width // TILE, partial(k), 0)
+        for far in (16, 15, -15, 11, -11):
+            travel(far, k).start()
 
     def outputs(k, carry):
         outs[k] = dot(ph[k], wd[k]).astype(BF16)
@@ -386,9 +391,8 @@
     finish(0)
     relay(3, -3)
     finish(1)
-    total = add_up(0)
-    for i in range(2):
-        down_ref[i] = total[:, i * hid : (i + 1) * hid]
+    for k in range(2):
+        down_ref[k] = add_up(0, k)
 
     for t in range(2):
         for rp in range(SIDE):
@@ -402,7 +406,8 @@
             to_line(t, r).wait_send()
             to_block(t, r).wait_send()
     for far in NEXT:
-        travel(far).wait_send()
+        travel(far, 0).wait_send()
+        travel(far, 1).wait_send()
 
 
 def hand_over(*refs):
@@ -454,8 +459,8 @@
             pltpu.VMEM((reach, SIDE * rows, width), BF16),
             pltpu.VMEM((reach, rows, width), BF16),
             pltpu.VMEM((reach, rows, width), BF16),
-            pltpu.VMEM((width, mine * hid), BF16),
-            pltpu.VMEM((len(NEXT), share, mine * hid), BF16),
+            pltpu.VMEM((mine, width, hid), BF16),
+            pltpu.VMEM((len(NEXT), mine, share, hid), BF16),
             dma((4,)),
             dma((3,)),
             dma((2, SIDE, SIDE)),
@@ -468,8 +473,8 @@
             dma((2, reach)),
             dma((2, reach)),
             dma((2, reach)),
-            dma((len(NEXT),)),
-            dma((len(NEXT),)),
+            dma((len(NEXT), mine)),
+            dma((len(NEXT), mine)),
         ],
         compiler_params=pltpu.CompilerParams(
             collective_id=0, has_side_effects=True, vmem_limit_bytes=58 * 1024 * 1024

time: 85.6 us -> 85.4 us (level)
  the two profiles are of different devices: /device:TPU:96 before, /device:TPU:32 now
where the time goes in v5:
time: 85.4 us; the launch traced here: 85.2 us
  Pallas kernels  84.6 us (99%)
    pallas_call x1, Pallas kernels, on_device(): pl.pallas_call(lambda *refs: layer_kernel(n_dp, *refs), out_shape=(jax.Sh...  82.9 us

profile of v5, /device:TPU:32, one launch (start us, length us, event | category | flops | bytes accessed | tf_op | source)
XLA Modules:
  0.0 85.2 jit_solution(4685473160670673621)
XLA Ops:
  0.6 82.9 %shard_map.94 = (bf16[32,1024]{1,0:T(8,128)(2,1)}, bf16[32,1024]{1,0:T(8,128)(2,1)}, f32[2,32,384]{2,1,0:T(8,128)}) custom-call(bf16[32,1024]{1,0:T(8,128)(2,1)} %refs_0_.1, s32[8,32]{1,0:T(8,128)} %bitcast.3, f32[8,32]{1,0:T(8,128)} %bitcast.4, bf16[2,1024,384]{2,1,0:T(8,128)(2,1)} %refs_3_.1, bf16[2,1024,384]{2,1,0:T(8,128)(2,1)} %refs_4_.1, ...), custom_call_target="tpu_custom_call" | custom-call | tf_op jit(solution)/shard_map/pallas_call | solution.py:429
  83.6 1.7 %shard_map.95 = (bf16[32,1024]{1,0:T(8,128)(2,1)}, bf16[32,1024]{1,0:T(8,128)(2,1)}, f32[2,32,384]{2,1,0:T(8,128)}) custom-call(bf16[32,1024]{1,0:T(8,128)(2,1)} %get-tuple-element.9.refs_0_, bf16[32,1024]{1,0:T(8,128)(2,1)} %get-tuple-element.10.refs_1_, f32[2,32,384]{2,1,0:T(8,128)} %get-tuple-element.11.refs_2_), custom_call_target="tpu_custom_call" | custom-call | tf_op jit(solution)/shard_map/pallas_call | solution.py:484
